TPU v7x, 128 devices: a whole 4x4x4 slice. The times are simulated.
128 devices in a mesh: dev: 128 (over x, y, z, core).
Axes of the slice: x: 4, y: 4, z: 4, core: 2. Of those that a mesh axis runs over, the one named last changes fastest.
Arguments:
- stream: bfloat16 [16384, 1536], P('dev'), may hold values from -24 to 24
- attn_gain: bfloat16 [1536], P('dev'), may hold values from 0.5 to 1.5
- w_query: bfloat16 [1536, 1536], P('dev'), may hold values from -0.15625 to 0.15625
- w_key: bfloat16 [1536, 768], P('dev'), may hold values from -0.15625 to 0.15625
- w_value: bfloat16 [1536, 768], P('dev'), may hold values from -0.15625 to 0.15625
- w_out: bfloat16 [1536, 1536], P('dev'), may hold values from -0.625 to 0.625
- mlp_gain: bfloat16 [1536], P('dev'), may hold values from 0.5 to 1.5
- w_gate: bfloat16 [1536, 4096], P('dev'), may hold values from -0.15625 to 0.15625
- w_up: bfloat16 [1536, 4096], P('dev'), may hold values from -0.15625 to 0.15625
- w_down: bfloat16 [4096, 1536], P('dev'), may hold values from -0.09375 to 0.09375
- parent: int32 [128], replicated, may hold values from -1 to 127, as said below
- live_mask: int32 [16384], P('dev'), may hold values from 0 to 1, as said below
- cotangent: bfloat16 [16384, 1536], P('dev'), may hold values from -6 to 6
Outputs:
- mixed_out: bfloat16 [16384, 1536], P('dev')
- stream_grad: float32 [16384, 1536], P('dev')
- attn_gain_grad: float32 [1536], P('dev')
- w_query_grad: float32 [1536, 1536], P('dev')
- w_key_grad: float32 [1536, 768], P('dev')
- w_value_grad: float32 [1536, 768], P('dev')
- w_out_grad: float32 [1536, 1536], P('dev')
- mlp_gain_grad: float32 [1536], P('dev')
- w_gate_grad: float32 [1536, 4096], P('dev')
- w_up_grad: float32 [1536, 4096], P('dev')
- w_down_grad: float32 [4096, 1536], P('dev')
- stream_rms: float32 [16384], P('dev')
- branch_rms: float32 [16384], P('dev')
Inputs may be any that keep to these rules, and one draw needn't show every extreme that they name: parent[b] is the block before b in its tree, or -1. There are 6 trees of 20 blocks: a chain of 8 trunk blocks, 4 branch blocks whose parent is the last trunk block, and 2 leaf blocks under each branch. All other blocks are padding, with parent -1 and no children. A tree's blocks may stand at any block indices. `live_mask`: every token of a trunk or branch block is 1, every token of a padding block 0; in a leaf block the 1s come first.
All inputs are finite; a program needn't handle non-finite values.
Results may differ from a plain program's by a relative error of at most 0.015.
Values may be sent and summed in bfloat16 or wider, within the bound.
A program may use at most 576 MiB of HBM per device.

v0:
```python
import functools

import jax
import jax.numpy as jnp
import numpy as np
from jax import lax
from jax.experimental import pallas as pl
from jax.experimental.pallas import tpu as pltpu
from jax.sharding import PartitionSpec as P

HEADS = 16
KV_HEADS = 8
HEAD_DIM = 96
BLOCK = 128
DEPTH = 10
D = 1536
FF = 4096
MEMBERS = 8
LANES = 128

EPSILON = 1e-05
ROPE_BASE = 100000.0
NEGATIVE = -1e30
SCALE = HEAD_DIM ** (-0.5)
MESH = pl.DeviceIdType.MESH
BF16 = jnp.bfloat16
F32 = jnp.float32
VMEM_BYTES = 56 * 2**20


def spot():
    me = lax.axis_index("dev")
    return me // 32, (me // 8) % 4, (me // 2) % 4, me % 2


def device_of(x, y, z, c):
    return ((x % 4) * 4 + (y % 4)) * 8 + (z % 4) * 2 + c


def announce(peers):
    barrier = pltpu.get_barrier_semaphore()
    for peer in peers:
        pl.semaphore_signal(barrier, inc=1, device_id=(peer,), device_id_type=MESH)


def await_peers(peers):
    pl.semaphore_wait(pltpu.get_barrier_semaphore(), len(peers))


def axis_peers(x, y, z, c, far):
    steps = (1, 2, 3) if far else (1, 3)
    return [device_of(x + k, y, z, c) for k in steps] + [device_of(x, y + k, z, c) for k in steps]


def group_peer(x, y, z, c, k):
    member = (z * 2 + c + k) % MEMBERS
    return (x * 4 + y) * MEMBERS + member


class Wire:
    def __init__(self, send_sems, recv_sems):
        self.send_sems = send_sems
        self.recv_sems = recv_sems
        self.used = 0
        self.open = []

    def reserve(self, count):
        self.used += count
        return self.used - count

    def make(self, slot, source, target, peer):
        return pltpu.make_async_remote_copy(
            src_ref=source,
            dst_ref=target,
            send_sem=self.send_sems.at[slot],
            recv_sem=self.recv_sems.at[slot],
            device_id=(peer,),
            device_id_type=MESH,
        )

    def send(self, source, target, peer):
        copy = self.make(self.reserve(1), source, target, peer)
        copy.start()
        self.open.append(copy)
        return copy

    def close(self):
        for copy in self.open:
            copy.wait_send()
        self.open = []


class Ring:
    def __init__(self, wire, own, part, place, up, down):
        self.wire, self.own, self.part = wire, own, part
        self.place, self.up, self.down = place, up, down

    def begin(self):
        send, part, place = self.wire.send, self.part, self.place
        self.low_up = send(self.own(0), part(place, 0), self.up)
        self.high_down = send(self.own(1), part(place, 1), self.down)
        self.high_up = send(self.own(1), part(place, 1), self.up)
        self.low_down = send(self.own(0), part(place, 0), self.down)

    def relay(self):
        before, after = (self.place + 3) % 4, (self.place + 1) % 4
        self.low_up.wait_recv()
        self.far_up = self.wire.send(self.part(before, 0), self.part(before, 0), self.up)
        self.high_down.wait_recv()
        self.far_down = self.wire.send(self.part(after, 1), self.part(after, 1), self.down)

    def near(self):
        self.high_up.wait_recv()
        self.low_down.wait_recv()

    def far(self):
        self.far_up.wait_recv()
        self.far_down.wait_recv()


class PlaneGather:
    def __init__(self, wire, own, out, cut, xyzc):
        self.wire, self.own, self.out, self.cut = wire, own, out, cut
        x, y, z, c = xyzc
        self.x, self.y = x, y
        self.x_up, self.x_down = device_of(x + 1, y, z, c), device_of(x + 3, y, z, c)
        self.y_up, self.y_down = device_of(x, y + 1, z, c), device_of(x, y + 3, z, c)

    def pair(self, one_own, one_part, two_own, two_part, one_on_x):
        on_x = (self.x, self.x_up, self.x_down)
        on_y = (self.y, self.y_up, self.y_down)
        cut = self.cut.quarter
        self.one = Ring(
            self.wire,
            lambda side: one_own(cut(0, side)),
            lambda place, side: one_part(place, cut(0, side)),
            *(on_x if one_on_x else on_y),
        )
        self.two = Ring(
            self.wire,
            lambda side: two_own(cut(1, side)),
            lambda place, side: two_part(place, cut(1, side)),
            *(on_y if one_on_x else on_x),
        )
        self.one.begin()
        self.two.begin()

    def first(self):
        own, out, x, y = self.own, self.out, self.x, self.y
        self.pair(
            lambda q: own.at[q],
            lambda place, q: out.at[(place, y) + q],
            lambda q: own.at[q],
            lambda place, q: out.at[(x, place) + q],
            True,
        )

    def relay(self):
        self.one.relay()
        self.two.relay()

    def near(self):
        self.one.near()
        self.two.near()

    def far(self):
        self.one.far()
        self.two.far()

    def settle(self):
        self.near()
        self.far()

    def second(self):
        out, x, y = self.out, self.x, self.y
        every = slice(None)
        self.pair(
            lambda q: out.at[(every, y) + q],
            lambda place, q: out.at[(every, place) + q],
            lambda q: out.at[(x, every) + q],
            lambda place, q: out.at[(place, every) + q],
            False,
        )


class Rows:
    def __init__(self, rows, cols, start=0):
        self.rows, self.cols, self.start = rows // 2, cols // 2, start

    def half(self, half):
        return (pl.ds(half * self.rows, self.rows),)

    def side(self, side):
        return (slice(None), pl.ds(side * self.cols, self.cols))

    def quarter(self, half, side):
        first = self.start + side * self.cols
        if not isinstance(first, int):
            first = pl.multiple_of(first, LANES)
        return self.half(half) + (pl.ds(first, self.cols),)

    def shapes(self):
        return (self.rows, 2 * self.cols), (self.rows, self.cols)


class Units:
    def half(self, half):
        return (pl.ds(half * 6, 6),)

    def side(self, side):
        return (pl.ds(side * 3, 3),)

    def quarter(self, half, side):
        return (pl.ds(half * 6 + side * 3, 3),)

    def shapes(self):
        return (6, BLOCK, LANES), (3, BLOCK, LANES)


class GroupGather:
    def __init__(self, wire, own, out, xyzc):
        self.wire, self.own, self.out = wire, own, out
        x, y, z, c = xyzc
        self.z, self.c = z, c
        self.sibling = device_of(x, y, z, 1 - c)
        half = out.shape[2] // 2
        self.ring = Ring(
            wire,
            lambda side: own.at[pl.ds(side * half, half)],
            lambda place, side: out.at[place, c, pl.ds(side * half, half)],
            z, device_of(x, y, z + 1, c), device_of(x, y, z + 3, c),
        )
        self.crossed = []

    def begin(self):
        self.ring.begin()
        self.crossed.append(self.wire.send(self.own, self.out.at[self.z, self.c], self.sibling))

    def cross(self, k):
        piece = self.out.at[(self.z + k) % 4, self.c]
        self.crossed.append(self.wire.send(piece, piece, self.sibling))

    def relay(self):
        self.ring.relay()

    def near(self):
        self.ring.near()
        self.cross(1)
        self.cross(3)

    def far(self):
        self.ring.far()
        self.cross(2)

    def finish(self, after=0):
        for copy in self.crossed[after:]:
            copy.wait_recv()


class SecondRound:
    def __init__(self, wire, summed, second_in, xyzc):
        self.wire, self.summed, self.second_in = wire, summed, second_in
        self.x, self.y, self.z, self.c = xyzc

    def peer(self, along_x, k):
        if along_x:
            return device_of(self.x + k, self.y, self.z, self.c)
        return device_of(self.x, self.y + k, self.z, self.c)

    def place(self, half, k):
        return ((self.x, self.y)[half] + k) % 4

    def second(self):
        self.copies = []
        for k in (2, 1, 3):
            for half in range(2):
                self.copies.append(
                    self.wire.send(
                        self.summed.at[half, self.place(1 - half, k)],
                        self.second_in.at[half, k - 1],
                        self.peer(half == 1, k),
                    )
                )

    def total(self, half):
        total = self.summed[half, self.place(1 - half, 0)].astype(F32)
        for k in range(3):
            total = total + self.second_in[half, k].astype(F32)
        return total

    def arrive(self):
        for copy in self.copies:
            copy.wait_recv()


class PlaneScatter(SecondRound):
    def __init__(self, wire, terms, cut, scratch, xyzc):
        *room, self.near_in, self.far_in, self.passed, summed, second_in = scratch
        super().__init__(wire, summed, second_in, xyzc)
        self.terms, self.cut, self.room = terms, cut, room

    def lead(self, half, k, line=slice(None)):
        place = self.place(half, k)
        return (place, line) if half == 0 else (line, place)

    def part(self, half, k, side):
        return self.terms.at[self.lead(half, k) + self.cut.quarter(half, side)]

    def own(self, half, line):
        if self.room:
            return self.room[0][half, line]
        return self.terms[self.lead(half, 0, line) + self.cut.half(half)]

    def edge(self, half, way, line):
        if self.room:
            return self.room[1][half, way, line]
        return self.terms[self.lead(half, (1, 3)[way], line) + self.cut.quarter(half, way)]

    def first(self):
        send = self.wire.send
        self.far, self.plain, self.locals = [], [], []
        if self.room:
            sems = self.room[2]
            for half in range(2):
                pairs = [(self.terms.at[self.lead(half, 0) + self.cut.half(half)], self.room[0].at[half])]
                pairs += [(self.part(half, (1, 3)[way], way), self.room[1].at[half, way]) for way in range(2)]
                for slot, (source, target) in enumerate(pairs):
                    copy = pltpu.make_async_copy(source, target, sems.at[half, slot])
                    copy.start()
                    self.locals.append(copy)
        for half in range(2):
            for way in range(2):
                self.far.append(
                    send(self.part(half, 2, way), self.far_in.at[half, way], self.peer(half == 0, (1, 3)[way]))
                )
        for half in range(2):
            for way in range(2):
                k = (1, 3)[way]
                landing = self.near_in.at[(half, way, slice(None)) + self.cut.side(1 - way)]
                self.plain.append(send(self.part(half, k, 1 - way), landing, self.peer(half == 0, k)))

    def relay(self):
        for copy in self.locals:
            copy.wait()
        self.relayed = []
        for half in range(2):
            for way in range(2):
                self.far[half * 2 + way].wait_recv()

                def add(line, carry):
                    total = self.edge(half, way, line).astype(F32) + self.far_in[half, way, line].astype(F32)
                    self.passed[half, way, line] = total.astype(BF16)
                    return carry

                lax.fori_loop(0, 4, add, 0)
                landing = self.near_in.at[(half, way, slice(None)) + self.cut.side(way)]
                self.relayed.append(
                    self.wire.send(self.passed.at[half, way], landing, self.peer(half == 0, (1, 3)[way]))
                )

    def add_first(self):
        for copy in self.plain + self.relayed:
            copy.wait_recv()
        for half in range(2):

            def body(line, carry):
                total = self.own(half, line).astype(F32)
                for way in range(2):
                    total = total + self.near_in[half, way, line].astype(F32)
                self.summed[half, line] = total.astype(BF16)
                return carry

            lax.fori_loop(0, 4, body, 0)


def scatter_scratch(cut, room=False):
    half, part = cut.shapes()
    vmem = pltpu.VMEM
    held = [vmem((2, 4) + half, BF16), vmem((2, 2, 4) + part, BF16), pltpu.SemaphoreType.DMA((2, 3))]
    return (held if room else []) + [
        vmem((2, 2, 4) + half, BF16),
        vmem((2, 2, 4) + part, BF16),
        vmem((2, 2, 4) + part, BF16),
        vmem((2, 4) + half, BF16),
        vmem((2, 3) + half, BF16),
    ]


class GroupScatter:
    def __init__(self, wire, terms, mine, crossed_in, summed, ring_in, local_sem, xyzc):
        self.wire, self.terms = wire, terms
        self.mine, self.crossed_in, self.summed, self.ring_in = mine, crossed_in, summed, ring_in
        self.x, self.y, self.z, self.c = xyzc
        self.local_sem = local_sem

    def begin(self):
        self.local = pltpu.make_async_copy(self.terms.at[:, self.c], self.mine, self.local_sem)
        self.local.start()
        sibling = device_of(self.x, self.y, self.z, 1 - self.c)
        self.crossed = {}
        for k in (2, 1, 3, 0):
            place = (self.z + k) % 4
            self.crossed[k] = self.wire.send(
                self.terms.at[place, 1 - self.c], self.crossed_in.at[place], sibling
            )

    def turn(self):
        self.local.wait()
        self.copies = []
        for k in (2, 1, 3):
            place = (self.z + k) % 4
            self.crossed[k].wait_recv()

            def body(tile, carry):
                total = self.mine[place, tile].astype(F32) + self.crossed_in[place, tile].astype(F32)
                self.summed[place, tile] = total.astype(BF16)
                return carry

            lax.fori_loop(0, 12, body, 0)
            self.copies.append(
                self.wire.send(
                    self.summed.at[place],
                    self.ring_in.at[k - 1],
                    device_of(self.x, self.y, self.z + k, self.c),
                )
            )

    def finish(self, out):
        self.crossed[0].wait_recv()
        for copy in self.copies:
            copy.wait_recv()
        for tile in range(12):
            total = self.mine[self.z, tile].astype(F32) + self.crossed_in[self.z, tile].astype(F32)
            for k in range(3):
                total = total + self.ring_in[k, tile].astype(F32)
            out[:, tile * LANES : (tile + 1) * LANES] = total


class ChipScatter:
    def __init__(self, wire, terms, at, crossed_in, ring_in, xyzc):
        self.wire, self.terms, self.at = wire, terms, at
        self.crossed_in, self.ring_in = crossed_in, ring_in
        self.x, self.y, self.z, self.c = xyzc
        self.crossed_slot, self.ring_slot = wire.reserve(4), wire.reserve(3)
        self.all_tiles = pl.ds(0, 12)

    def place(self, step):
        return (self.z + step) % 4

    def crossed(self, step):
        place = self.place(step)
        return self.wire.make(
            self.crossed_slot + step,
            self.terms.at[place, self.at + 1 - self.c, self.all_tiles],
            self.crossed_in.at[place],
            device_of(self.x, self.y, self.z, 1 - self.c),
        )

    def ring(self, step):
        return self.wire.make(
            self.ring_slot + step - 1,
            self.terms.at[self.place(step), self.at + self.c, self.all_tiles],
            self.ring_in.at[step - 1],
            device_of(self.x, self.y, self.z + step, self.c),
        )

    def put(self, step, grads):
        place = self.place(step)
        for core in range(2):
            for tile in range(12):
                self.terms[place, self.at + core, tile] = grads[
                    core * BLOCK : (core + 1) * BLOCK, tile * LANES : (tile + 1) * LANES
                ]
        self.crossed(step).start()

    def turn(self, step):
        place, line = self.place(step), self.at + self.c
        self.crossed(step).wait_recv()

        def add(tile, carry):
            total = self.terms[place, line, tile].astype(F32) + self.crossed_in[place, tile].astype(F32)
            self.terms[place, line, tile] = total.astype(BF16)
            return carry

        lax.fori_loop(0, 12, add, 0)
        self.ring(step).start()

    def total(self):
        self.crossed(0).wait_recv()
        for step in range(1, 4):
            self.ring(step).wait_recv()
        tiles = []
        for tile in range(12):
            total = self.terms[self.z, self.at + self.c, tile].astype(F32)
            total = total + self.crossed_in[self.z, tile].astype(F32)
            for step in range(3):
                total = total + self.ring_in[step, tile].astype(F32)
            tiles.append(total)
        return jnp.concatenate(tiles, axis=1)

    def close(self):
        for step in range(4):
            self.crossed(step).wait_send()
        for step in range(1, 4):
            self.ring(step).wait_send()


class RingScatter(ChipScatter):
    def __init__(self, wire, terms, crossed_in, near_in, far_in, xyzc):
        super().__init__(wire, terms, 0, crossed_in, None, xyzc)
        self.near_in, self.far_in = near_in, far_in
        self.moved = []

    def sum_tiles(self, place, tiles, extra=None):
        def add(tile, carry):
            total = self.terms[place, self.c, tile].astype(F32)
            if extra is None:
                total = total + self.crossed_in[place, tile].astype(F32)
            else:
                total = total + self.far_in[extra, tile - extra * 6].astype(F32)
            self.terms[place, self.c, tile] = total.astype(BF16)
            return carry

        lax.fori_loop(*tiles, add, 0)

    def move(self, place, first, landing, k):
        source = self.terms.at[place, self.c, pl.ds(first, 6)]
        copy = self.wire.send(source, landing, device_of(self.x, self.y, self.z + k, self.c))
        self.moved.append(copy)
        return copy

    def turn(self, step):
        place = self.place(step)
        self.crossed(step).wait_recv()
        self.sum_tiles(place, (0, 12))
        if step == 2:
            self.far = [self.move(place, 6 * way, self.far_in.at[way], (1, 3)[way]) for way in range(2)]
        else:
            way = (1, 3).index(step)
            plain = 6 * (1 - way)
            self.move(place, plain, self.near_in.at[way, pl.ds(plain, 6)], step)

    def pass_on(self, step):
        way = (1, 3).index(step)
        place = self.place(step)
        self.far[way].wait_recv()
        self.sum_tiles(place, (6 * way, 6 * way + 6), way)
        self.move(place, 6 * way, self.near_in.at[way, pl.ds(6 * way, 6)], step)

    def total(self):
        self.crossed(0).wait_recv()
        for copy in self.moved[2:]:
            copy.wait_recv()
        tiles = []
        for tile in range(12):
            total = self.terms[self.z, self.c, tile].astype(F32) + self.crossed_in[self.z, tile].astype(F32)
            for way in range(2):
                total = total + self.near_in[way, tile].astype(F32)
            tiles.append(total)
        return jnp.concatenate(tiles, axis=1)

    def close(self):
        for step in range(4):
            self.crossed(step).wait_send()


def group_scatter_scratch():
    return [
        pltpu.VMEM((4, 12, BLOCK, LANES), BF16),
        pltpu.VMEM((4, 12, BLOCK, LANES), BF16),
        pltpu.VMEM((4, 12, BLOCK, LANES), BF16),
        pltpu.VMEM((3, 12, BLOCK, LANES), BF16),
        pltpu.SemaphoreType.DMA,
    ]


def chip_scatter_scratch():
    return [pltpu.VMEM((4, 12, BLOCK, LANES), BF16), pltpu.VMEM((3, 12, BLOCK, LANES), BF16)]


def wire_scratch(count):
    return [pltpu.SemaphoreType.DMA((count,)), pltpu.SemaphoreType.DMA((count,))]


ANY = pl.BlockSpec(memory_space=pl.ANY)
INVMEM = pl.BlockSpec(memory_space=pltpu.VMEM)


def communicate(kernel, out_shapes, in_specs, out_specs, scratch, ident, name, vmem=VMEM_BYTES):
    return pl.pallas_call(
        kernel,
        out_shape=out_shapes,
        in_specs=in_specs,
        out_specs=out_specs,
        scratch_shapes=scratch,
        compiler_params=pltpu.CompilerParams(
            collective_id=ident, has_side_effects=True, vmem_limit_bytes=vmem
        ),
        name=name,
    )


def key_unit(member):
    return member + jnp.where(member >= 6, 6, 0) + jnp.where(member >= 7, 1, 0)


def value_unit(member):
    return member + 6 + jnp.where(member >= 6, 1, 0) + jnp.where(member >= 7, 1, 0)


def gain_rows(pieces):
    return jnp.concatenate(join_heads(pieces), axis=1)


def head_window(tiles, head):
    tile, skip = divmod(head * HEAD_DIM, LANES)
    lane = lane_of(tiles[0].shape)
    window = pltpu.roll(tiles[tile], (LANES - skip) % LANES, 1)
    if skip + HEAD_DIM > LANES:
        window = jnp.where(lane < LANES - skip, window, pltpu.roll(tiles[tile + 1], LANES - skip, 1))
    return jnp.where(lane < HEAD_DIM, window, 0.0)


def join_heads(pieces):
    lane = lane_of(pieces[0].shape)
    tiles = []
    for tile in range(len(pieces) * 3 // 4):
        piece, skip = divmod(tile * LANES, HEAD_DIM)
        low = pltpu.roll(pieces[piece], (LANES - skip) % LANES, 1)
        high = pltpu.roll(pieces[piece + 1], HEAD_DIM - skip, 1)
        tiles.append(jnp.where(lane < HEAD_DIM - skip, low, high))
    return tiles


def mix_groups(parts):
    group = lane_of(parts[0][0].shape) // 32
    mixed = None
    for i, (tile, g) in enumerate(parts):
        turned = pltpu.roll(tile, (32 * (i - g)) % LANES, 1)
        mixed = turned if mixed is None else jnp.where(group == i, turned, mixed)
    return mixed


def lane_of(shape):
    return lax.broadcasted_iota(jnp.int32, shape, len(shape) - 1)


def pack_tile(unit, extra, place):
    return jnp.where(lane_of(unit.shape) < HEAD_DIM, unit, pltpu.roll(extra, (96 - 32 * place) % LANES, 1))


def unpack_extra(tiles):
    lane = lane_of(tiles[0].shape)
    extra = jnp.where(lane < 32, pltpu.roll(tiles[0], 32, 1), 0.0)
    extra = jnp.where(jnp.logical_and(lane >= 32, lane < 64), pltpu.roll(tiles[1], 64, 1), extra)
    return jnp.where(jnp.logical_and(lane >= 64, lane < 96), pltpu.roll(tiles[2], 96, 1), extra)


def swap_halves(rows):
    lane = lane_of(rows.shape)
    return jnp.where(lane < HEAD_DIM // 2, pltpu.roll(rows, LANES - 48, 1), pltpu.roll(rows, 48, 1))


def rope_table():
    half = HEAD_DIM // 2
    frequency = ROPE_BASE ** (-2.0 * np.arange(half, dtype=np.float64) / HEAD_DIM)
    frequency = frequency.astype(np.float32)
    places = np.arange(DEPTH * BLOCK, dtype=np.float32)
    angles = (places[:, None] * frequency[None, :]).astype(np.float64)
    table = np.zeros((DEPTH * BLOCK, LANES), np.float32)
    table[:, :half] = np.cos(angles)
    table[:, half:HEAD_DIM] = np.sin(angles)
    return jnp.asarray(table.reshape(DEPTH, BLOCK, LANES))


def turning(table):
    lane = lane_of(table.shape)
    cosine = jnp.where(lane < 48, table, pltpu.roll(table, 48, 1))
    sine = jnp.where(lane < 48, -pltpu.roll(table, LANES - 48, 1), jnp.where(lane < HEAD_DIM, table, 0.0))
    return cosine, sine


def count_ancestors(lineage, block):
    count = jnp.int32(0)
    for step in range(DEPTH):
        count = count + jnp.where(lineage[block, step] >= 0, 1, 0)
    return count


def write_lineage(parent, first, lineage):
    def one(block, carry):
        def hop(step, node):
            lineage[block, step] = node
            above = parent[jnp.maximum(node, 0)]
            return jnp.where(node >= 0, above, -1)

        lax.fori_loop(0, DEPTH, hop, first + block)
        return carry

    lax.fori_loop(0, MEMBERS, one, 0)


def attend_block(lineage, block, queries, alive, load, scores):
    limit = count_ancestors(lineage, block)
    t = lax.broadcasted_iota(jnp.int32, (2 * BLOCK, BLOCK), 0) % BLOCK
    u = lax.broadcasted_iota(jnp.int32, (2 * BLOCK, BLOCK), 1)
    own = jnp.logical_and(u <= t, jnp.logical_or(alive > 0.5, u == t))
    nodes = [jnp.maximum(lineage[block, step], 0) for step in range(DEPTH)]
    pairs = range(0, DEPTH, 2)
    highest = None
    for step in pairs:
        keys = jnp.concatenate([load(node, key_unit(lax.rem(node, 8))) for node in nodes[step : step + 2]], axis=0)
        part = lax.dot_general(queries, keys, (((1,), (1,)), ((), ())), preferred_element_type=F32) * SCALE
        near = part[:, :BLOCK]
        if step == 0:
            near = jnp.where(own, near, NEGATIVE)
        else:
            near = near + jnp.where(step < limit, 0.0, NEGATIVE)
        far = part[:, BLOCK:] + jnp.where(step + 1 < limit, 0.0, NEGATIVE)
        scores[step] = near
        scores[step + 1] = far
        both = jnp.maximum(near, far)
        highest = both if step == 0 else jnp.maximum(highest, both)
    largest = jnp.max(highest, axis=1, keepdims=True)
    totals = jnp.zeros((2 * BLOCK, BLOCK), F32)
    attended = jnp.zeros((2 * BLOCK, LANES), F32)
    for step in pairs:
        near, far = jnp.exp(scores[step] - largest), jnp.exp(scores[step + 1] - largest)
        totals = totals + near + far
        values = jnp.concatenate(
            [load(node, value_unit(lax.rem(node, 8))) for node in nodes[step : step + 2]], axis=0
        )
        terms = jnp.concatenate([near.astype(BF16), far.astype(BF16)], axis=1)
        attended = attended + jnp.dot(terms, values, preferred_element_type=F32)
    total = jnp.sum(totals, axis=1, keepdims=True)
    return (attended / total).astype(BF16), largest + jnp.log(total)


def start_kernel(
    parent, table, stream, w_query, w_key, w_value, w_gate, w_up, w_out, small_rows, live_row, cotangent, own_down,
    lineage, live, gains, query, stream_all, attn_all,
    kv_out, middle, rms_out, grad_middle, grads_in, down_terms, feed_lines, wide_lines, out_terms, gain_terms,
    attended_out, log_rows,
    packed, out_low, small, stage, packed_in, out_in, small_in, wide_tall, wide_own, out_own, gain_own, gains_all,
    w_attn, own_kv, kv, w_out_all, w_feed, w_down, mid_all, cot_all, crossed_in, ring_in,
    att_out, att_in, att_pad, grads_out, *scratch,
):
    feed_scratch, wide_scratch = scratch[:5], scratch[5:10]
    send_sems, recv_sems, local_sems = scratch[10:]
    xyzc = x, y, z, c = spot()
    j = z * 2 + c
    base = (x * 4 + y) * MEMBERS
    sibling = device_of(x, y, z, 1 - c)
    wire = Wire(send_sems, recv_sems)
    group = [group_peer(x, y, z, c, k) for k in range(1, MEMBERS)]
    across, down_first = (((1,), (1,)), ((), ())), (((0,), (0,)), ((), ()))
    locals_ = []

    peers = group + axis_peers(x, y, z, c, True)
    announce(peers)

    stage[...] = jnp.zeros((16, FF), F32)
    wide_tall[96:] = jnp.zeros((8, 1536), F32)

    def staged(weights):
        width = weights.shape[1]
        stage[:12, :width] = weights[...].astype(F32)
        return [stage[:, tile * LANES : (tile + 1) * LANES] for tile in range(width // LANES)]

    def put_packed(member, tile, value):
        packed[member, :, tile * LANES : (tile + 1) * LANES] = value.astype(BF16)

    tiles = staged(w_query)
    for head in range(HEADS):
        put_packed(head // 2, head % 2, head_window(tiles, head))
    for place, weights in ((2, w_key), (3, w_value)):
        tiles = staged(weights)
        for member in range(MEMBERS):
            put_packed(member, place, head_window(tiles, member))
    for place, weights in ((4, w_gate), (8, w_up)):
        tiles = staged(weights)
        for member in range(MEMBERS):
            for tile in range(4):
                parts = [(tiles[2 * (4 * tile + i) + member // 4], member % 4) for i in range(4)]
                put_packed(member, place + tile, mix_groups(parts))
    out_low[...] = jnp.concatenate(staged(w_out), axis=1).astype(BF16)
    rows = pltpu.roll(small_rows[...], 12 * j, 1)
    live_rows = jnp.broadcast_to(live_row[...].astype(F32), (8, LANES))
    rows = jnp.where(lax.broadcasted_iota(jnp.int32, (8, LANES), 0) == 2, live_rows, rows)
    small[...] = jnp.concatenate([rows, jnp.zeros((8, LANES), F32)], axis=0).astype(BF16)
    await_peers(peers)

    def keep(source, target):
        copy = pltpu.make_async_copy(source, target, local_sems.at[len(locals_)])
        copy.start()
        locals_.append(copy)
        return copy

    def to_members(source, target):
        return [wire.send(source((j + k) % MEMBERS), target.at[j], group[k - 1]) for k in range(1, MEMBERS)]

    def half_of(member):
        return pl.ds(pl.multiple_of((member % 2) * 768, 768), 768)

    own_half = half_of(c)
    attn_part, feed_part = pl.ds(0, 512), pl.ds(512, 1024)
    attn_dealt = to_members(lambda member: packed.at[member, :, attn_part], packed_in.at[:, :, attn_part])
    small_dealt = to_members(lambda member: small, small_in)
    streams = GroupGather(wire, stream, mid_all, xyzc)
    streams.begin()
    first_kept = (keep(packed.at[j], packed_in.at[j]), keep(small, small_in.at[j]))
    out_kept = keep(out_low.at[:, own_half], out_in.at[j])
    stream_kept = keep(stream, mid_all.at[z, c])
    write_lineage(parent, base, lineage)
    for line in range(16):
        w_out_all[line // 4, line % 4, 96:] = jnp.zeros((32, D), BF16)

    for copy in attn_dealt + small_dealt:
        copy.wait_recv()
    out_dealt = to_members(lambda member: out_low.at[:, half_of(member)], out_in)
    feed_dealt_in = to_members(lambda member: packed.at[member, :, feed_part], packed_in.at[:, :, feed_part])
    for copy in first_kept:
        copy.wait()
    for member in range(MEMBERS):
        wide_tall[pl.ds(member * 12, 12), :512] = packed_in[member, :, :512].astype(F32)[:12]
    wide_own[:, :512] = wide_tall[:96, :512].astype(BF16)
    gain = small_in[0].astype(F32)
    for member in range(MEMBERS):
        row = small_in[member].astype(F32)
        live[member] = row[2:3]
        if member:
            gain = gain + row
    gain_own[...] = gain.astype(BF16)
    own_attn, own_feed = wide_own.at[:, pl.ds(0, 512)], wide_own.at[:, pl.ds(512, 1024)]
    attn = PlaneGather(wire, own_attn, w_attn, Rows(96, 512), xyzc)
    attn.first()
    tiny = [wire.send(gain_own, gains_all.at[x, y], device_of(x + k, y, z, c)) for k in range(1, 4)]
    attn_kept = keep(own_attn, w_attn.at[x, y])
    gain_kept = keep(gain_own, gains_all.at[x, y])
    down_kept = keep(own_down, w_down.at[x, y])

    attn.relay()
    streams.relay()
    gain_kept.wait()
    for copy in tiny:
        copy.wait_recv()
    line = gains_all.at[:, y]
    tiny = [wire.send(line, line, device_of(x, y + k, z, c)) for k in range(1, 4)]
    attn_kept.wait()
    attn.settle()
    attn.second()
    for copy in out_dealt:
        copy.wait_recv()
    out_kept.wait()
    for member in range(MEMBERS):
        wide_tall[pl.ds(member * 12, 12), :768] = out_in[member].astype(F32)[:12]
    out_own[...] = wide_tall[:96, :768].astype(BF16)
    out_kept = keep(out_own, w_out_all.at[x, y, pl.ds(0, 96), own_half])
    out_kept.wait()
    outs = PlaneGather(wire, w_out_all.at[x, y], w_out_all, Rows(96, 768, c * 768), xyzc)
    outs.first()
    for copy in feed_dealt_in:
        copy.wait_recv()
    for member in range(MEMBERS):
        wide_tall[pl.ds(member * 12, 12), 512:] = packed_in[member, :, 512:].astype(F32)[:12]
    wide_own[:, 512:] = wide_tall[:96, 512:].astype(BF16)
    feed_kept = keep(own_feed, w_feed.at[x, y])
    streams.near()
    streams.far()
    attn.relay()
    outs.relay()
    for copy in tiny:
        copy.wait_recv()
    pieces = [gains_all[piece // 4, piece % 4].astype(F32)[:8] for piece in range(16)]
    gains[...] = gain_rows(pieces)
    attn.settle()
    stream_kept.wait()
    streams.finish()
    attn_copied = keep(w_attn, attn_all)
    stream_copied = keep(mid_all, stream_all)

    def project(step, carry):
        wide = mid_all[step].reshape(2 * BLOCK, D).astype(F32)
        rms = jnp.sqrt(jnp.mean(wide * wide, axis=1, keepdims=True) + EPSILON)
        rows = (wide * (1.0 / rms) * gains[0:1]).astype(BF16)
        raw = jnp.dot(rows, w_attn[...].reshape(D, 512), preferred_element_type=F32)
        for part in range(2):
            block = step * 2 + part
            depth = count_ancestors(lineage, block) - 1
            cos, sin = turning(table[depth])

            def turn(head):
                v = raw[part * BLOCK : (part + 1) * BLOCK, head * LANES : (head + 1) * LANES]
                return (v * cos + swap_halves(v) * sin).astype(BF16)

            query[block, :BLOCK] = turn(0)
            query[block, BLOCK:] = turn(1)
            kv[x, y, key_unit(block)] = turn(2)
            kv[x, y, value_unit(block)] = raw[part * BLOCK : (part + 1) * BLOCK, 3 * LANES :].astype(BF16)
        return carry

    lax.fori_loop(0, 2, project, 0)
    outs.settle()
    outs.second()
    lax.fori_loop(2, 4, project, 0)
    for tile in range(12):
        extra = kv[x, y, 12 + tile // 3].astype(F32)
        own_kv[tile] = pack_tile(kv[x, y, tile].astype(F32), extra, tile % 3).astype(BF16)

    pairs = PlaneGather(wire, own_kv, kv, Units(), xyzc)
    pairs.first()
    outs.relay()
    kept = keep(own_kv, kv.at[x, y, pl.ds(0, 12)])
    cotangents = GroupGather(wire, cotangent, cot_all, xyzc)
    cotangents.begin()
    cot_kept = keep(cotangent, cot_all.at[z, c])
    pairs.relay()
    kept.wait()
    outs.settle()
    swap_part = w_out_all.at[:, :, pl.ds(0, 96), own_half]
    swapped = wire.send(swap_part, swap_part, sibling)
    pairs.settle()
    pairs.second()

    def unpack(index, carry):
        k, half, other, extra = index // 16, (index // 8) % 2, (index // 2) % 4, index % 2
        a = half * ((x + k) % 4) + (1 - half) * other
        b = half * other + (1 - half) * ((y + k) % 4)
        extra = extra + 2 * half
        tiles = [kv[a, b, extra * 3 + part].astype(F32) for part in range(3)]
        kv[a, b, 12 + extra] = unpack_extra(tiles).astype(BF16)
        return carry

    lax.fori_loop(0, 16, unpack, 0)
    cotangents.relay()
    cotangents.near()
    cotangents.far()
    pairs.relay()
    early, wire.open = wire.open, []
    feed = PlaneGather(wire, own_feed, w_feed, Rows(96, 1024), xyzc)
    down = PlaneGather(wire, own_down, w_down, Rows(32, D), xyzc)
    feed.first()
    down.first()
    pairs.near()
    lax.fori_loop(16, 32, unpack, 0)
    lax.fori_loop(48, 64, unpack, 0)
    pairs.far()
    lax.fori_loop(32, 48, unpack, 0)
    for copy in early:
        copy.wait_send()
    stream_copied.wait()
    attn_copied.wait()

    kv_copied = keep(kv, kv_out)

    att_slot = wire.reserve(MEMBERS - 1)

    def load(node, unit):
        return kv[lax.div(node, 32), lax.rem(lax.div(node, 8), 4), unit]

    def att_copy(k):
        block = (j + 1 + k) % MEMBERS
        return wire.make(att_slot + k, att_out.at[block], att_in.at[j], base + block)

    def attend_one(k, scores):
        block = (j + 1 + k) % MEMBERS
        attended, logs = attend_block(lineage, block, query[block], live[block], load, scores)
        log_rows[block] = jnp.transpose(jnp.broadcast_to(logs, (2 * BLOCK, LANES)))[:8]
        att_out[block, :, :LANES] = attended[:BLOCK]
        att_out[block, :, LANES:] = attended[BLOCK:]

    def attend_pairs(first, last):
        def both(one, two):
            def each(pair, carry):
                attend_one(2 * pair, one)
                attend_one(2 * pair + 1, two)
                return carry

            lax.fori_loop(first, last, each, 0)

        room = pltpu.VMEM((DEPTH, 2 * BLOCK, LANES), F32)
        pl.run_scoped(both, room, room)

        def give(k, carry):
            att_copy(k).start()
            return carry

        lax.fori_loop(2 * first, min(2 * last, MEMBERS - 1), give, 0)

    attend_pairs(0, 1)
    feed.relay()
    down.relay()
    attend_pairs(1, 2)
    feed_kept.wait()
    down_kept.wait()
    feed.settle()
    feed.second()
    down.settle()
    down.second()
    attend_pairs(2, 4)
    feed.relay()
    down.relay()
    att_in[j] = att_out[j]
    att_copied = keep(att_out, attended_out)
    att_recv = [att_copy(k) for k in range(MEMBERS - 1)]

    for copy in att_recv:
        copy.wait_recv()
    for member in range(MEMBERS):
        att_pad[:, member * 256 : (member + 1) * 256] = att_in[member]
    swapped.wait_recv()

    def project_out(step, carry):
        cols = pl.ds(pl.multiple_of(step * 512, 512), 512)
        weights = w_out_all[:, :, :, cols].reshape(16 * LANES, 512)
        branch = jnp.dot(att_pad[...], weights, preferred_element_type=F32)
        middle[:, cols] = stream[:, cols].astype(F32) + branch
        return carry

    lax.fori_loop(0, 3, project_out, 0)
    rms = jnp.sqrt(jnp.mean(middle[...] * middle[...], axis=1, keepdims=True) + EPSILON)
    rms_out[...] = jnp.transpose(jnp.broadcast_to(rms, (BLOCK, LANES)))[:1]
    mid_all[z, c] = (middle[...] / rms * gains[1:2]).astype(BF16)
    mids = GroupGather(wire, mid_all.at[z, c], mid_all, xyzc)
    mids.begin()
    mids.relay()
    feed.settle()
    down.settle()
    kv_copied.wait()
    cot_kept.wait()
    cotangents.finish()
    for k in range(MEMBERS - 1):
        att_copy(k).wait_send()

    grad_rows = ChipScatter(wire, kv, 2, crossed_in, ring_in, xyzc)

    def rest(acts, grad_feed, feed_terms, wide_terms):
        feed_back_half(
            xyzc, wire, group, keep, mids, grad_rows, mid_all, cot_all, w_feed, w_down, w_out_all, kv, middle, gains,
            att_pad, att_copied, grads_out, feed_scratch, wide_scratch,
            acts, grad_feed, feed_terms, wide_terms,
            grad_middle, grads_in, down_terms, feed_lines, wide_lines, out_terms, gain_terms,
        )

    pl.run_scoped(
        rest,
        pltpu.VMEM((4, 2 * BLOCK, 512), BF16),
        pltpu.VMEM((4, 2 * BLOCK, 1024), BF16),
        pltpu.VMEM((4, 4, 96, 1024), BF16),
        pltpu.VMEM((4, 4, 32, D), BF16),
    )


def feed_back_half(
    xyzc, wire, group, keep, mids, grad_rows, mid_all, cot_all, w_feed, w_down, w_out_all, kv, middle, gains,
    att_pad, att_copied, grads_out, feed_scratch, wide_scratch,
    acts, grad_feed, feed_terms, wide_terms,
    grad_middle, grads_in, down_terms, feed_lines, wide_lines, out_terms, gain_terms,
):
    x, y, z, c = xyzc
    j = z * 2 + c
    across, down_first = (((1,), (1,)), ((), ())), (((0,), (0,)), ((), ()))

    def feed_forward(step):
        place = grad_rows.place(step)
        rows = mid_all[place].reshape(2 * BLOCK, D)
        weights = w_feed[...].reshape(D, 1024)
        both = jnp.dot(rows, weights, preferred_element_type=F32)
        gate, up = both[:, :512], both[:, 512:]
        sigmoid = 0.5 * jnp.tanh(0.5 * gate) + 0.5
        silu = gate * sigmoid
        acts[place] = (silu * up).astype(BF16)
        cot = cot_all[place].reshape(2 * BLOCK, D)
        grad_act = lax.dot_general(cot, w_down[...].reshape(512, D), across, preferred_element_type=F32)
        grad_gate = grad_act * up * sigmoid * (1.0 + gate * (1.0 - sigmoid))
        grad_feed[place, :, :512] = grad_gate.astype(BF16)
        grad_feed[place, :, 512:] = (grad_act * silu).astype(BF16)

    def feed_back(step):
        place = grad_rows.place(step)
        weights = w_feed[...].reshape(D, 1024)
        grads = lax.dot_general(grad_feed[place], weights, across, preferred_element_type=F32)
        grad_rows.put(step, grads.astype(BF16))

    mids.crossed[0].wait_recv()
    feed_forward(0)
    feed_back(0)
    mids.near()
    mids.crossed[1].wait_recv()
    mids.crossed[2].wait_recv()

    def near_chunk(index, carry):
        step = 1 + 2 * index
        feed_forward(step)
        feed_back(step)

        @pl.when(index > 0)
        def _():
            grad_rows.turn(1)

        return carry

    lax.fori_loop(0, 2, near_chunk, 0)
    mids.far()
    mids.crossed[3].wait_recv()
    grad_rows.turn(3)
    feed_forward(2)

    def down_weights(step, carry):
        cols = pl.ds(pl.multiple_of(step * 128, 128), 128)
        left = acts[:, :, cols].reshape(MEMBERS * BLOCK, 128)
        right = cot_all[...].reshape(MEMBERS * BLOCK, D)
        total = lax.dot_general(left, right, down_first, preferred_element_type=F32)
        wide_terms[step] = total.astype(BF16).reshape(4, 32, D)
        return carry

    lax.fori_loop(0, 4, down_weights, 0)
    wides = PlaneScatter(wire, wide_terms, Rows(32, D), wide_scratch, xyzc)
    wides.first()
    feed_back(2)

    def feed_weights(step, carry):
        cols = pl.ds(pl.multiple_of(step * 384, 384), 384)
        left = mid_all[:, :, :, cols].reshape(MEMBERS * BLOCK, 384)
        right = grad_feed[...].reshape(MEMBERS * BLOCK, 1024)
        total = lax.dot_general(left, right, down_first, preferred_element_type=F32)
        feed_terms[step] = total.astype(BF16).reshape(4, 96, 1024)
        return carry

    lax.fori_loop(0, 2, feed_weights, 0)
    grad_rows.turn(2)
    lax.fori_loop(2, 4, feed_weights, 0)
    feeds = PlaneScatter(wire, feed_terms, Rows(96, 1024), feed_scratch, xyzc)
    feeds.first()
    wides.relay()

    def down_rows(place, carry):
        outs = jnp.dot(acts[place], w_down[...].reshape(512, D), preferred_element_type=F32).astype(BF16)
        for core in range(2):
            for tile in range(12):
                kv[place, core, tile] = outs[
                    core * BLOCK : (core + 1) * BLOCK, tile * LANES : (tile + 1) * LANES
                ]
        return carry

    lax.fori_loop(0, 4, down_rows, 0)
    down_copied = keep(kv.at[:, pl.ds(0, 2), pl.ds(0, 12)], down_terms)
    grad_mid = grad_rows.total()
    rms = jnp.sqrt(jnp.mean(middle[...] * middle[...], axis=1, keepdims=True) + EPSILON)
    scaled = middle[...] / rms
    gain_terms[...] = jnp.sum(grad_mid * scaled, axis=0, keepdims=True)
    weighted = grad_mid * gains[1:2]
    back = (weighted - scaled * jnp.mean(weighted * scaled, axis=1, keepdims=True)) / rms
    grad_middle[...] = cot_all[z, c].astype(F32) + back
    branch_grad = grad_middle[...].astype(BF16)

    def spread(step, carry):
        weights = w_out_all[step].reshape(4 * LANES, D)
        grads = lax.dot_general(branch_grad, weights, across, preferred_element_type=F32).astype(BF16)
        for part in range(2):
            grads_out[step * 2 + part] = grads[:, part * 256 : (part + 1) * 256]
        return carry

    lax.fori_loop(0, 4, spread, 0)
    kept = keep(grads_out.at[j], grads_in.at[j])
    dealt = [
        wire.send(grads_out.at[(j + k) % MEMBERS], grads_in.at[j], group[k - 1]) for k in (4, 5, 3, 2, 6, 7, 1)
    ]
    feeds.relay()

    def out_weights(step, carry):
        cols = pl.ds(pl.multiple_of(step * 512, 512), 512)
        total = lax.dot_general(att_pad[:, cols], branch_grad, down_first, preferred_element_type=F32)
        w_out_all[step] = total.astype(BF16).reshape(4, LANES, D)
        return carry

    lax.fori_loop(0, 4, out_weights, 0)
    out_copied = keep(w_out_all.at[:, :, pl.ds(0, 96)], out_terms)

    wides.add_first()
    wide_copied = keep(wides.summed, wide_lines)
    feeds.add_first()
    feed_copied = keep(feeds.summed, feed_lines)
    for copy in dealt:
        copy.wait_recv()
    for copy in (kept, down_copied, out_copied, att_copied, wide_copied, feed_copied):
        copy.wait()
    wire.close()
    grad_rows.close()


def start(
    parent, table, stream, w_query, w_key, w_value, w_gate, w_up, w_out, small_rows, live_row, cotangent, own_down
):
    shape, vmem = jax.ShapeDtypeStruct, pltpu.VMEM
    smem = pl.BlockSpec(memory_space=pltpu.SMEM)
    return communicate(
        start_kernel,
        (
            shape((MEMBERS, DEPTH), jnp.int32),
            shape((MEMBERS, 1, LANES), F32),
            shape((8, D), F32),
            shape((MEMBERS, 2 * BLOCK, LANES), BF16),
            shape((4, 2, BLOCK, D), BF16),
            shape((4, 4, 96, 512), BF16),
            shape((4, 4, 16, BLOCK, LANES), BF16),
            shape((BLOCK, D), F32),
            shape((1, LANES), F32),
            shape((BLOCK, D), F32),
            shape((MEMBERS, BLOCK, 2 * LANES), BF16),
            shape((4, 2, 12, BLOCK, LANES), BF16),
            shape((2, 4, 48, 1024), BF16),
            shape((2, 4, 16, D), BF16),
            shape((4, 4, 96, D), BF16),
            shape((1, D), F32),
            shape((MEMBERS, BLOCK, 2 * LANES), BF16),
            shape((MEMBERS, 8, 2 * BLOCK), F32),
        ),
        [smem] + [INVMEM] * 10 + [ANY] * 2,
        (smem,) + (INVMEM,) * 3 + (ANY,) * 3 + (INVMEM,) * 3 + (ANY,) * 5 + (INVMEM, ANY, INVMEM),
        [
            vmem((MEMBERS, 16, 1536), BF16),
            vmem((16, 1536), BF16),
            vmem((16, LANES), BF16),
            vmem((16, FF), F32),
            vmem((MEMBERS, 16, 1536), BF16),
            vmem((MEMBERS, 16, 768), BF16),
            vmem((MEMBERS, 16, LANES), BF16),
            vmem((104, 1536), F32),
            vmem((96, 1536), BF16),
            vmem((96, 768), BF16),
            vmem((16, LANES), BF16),
            vmem((4, 4, 16, LANES), BF16),
            vmem((4, 4, 96, 512), BF16),
            vmem((12, BLOCK, LANES), BF16),
            vmem((4, 4, 16, BLOCK, LANES), BF16),
            vmem((4, 4, LANES, D), BF16),
            vmem((4, 4, 96, 1024), BF16),
            vmem((4, 4, 32, D), BF16),
            vmem((4, 2, BLOCK, D), BF16),
            vmem((4, 2, BLOCK, D), BF16),
        ]
        + chip_scatter_scratch()
        + [
            vmem((MEMBERS, BLOCK, 2 * LANES), BF16),
            vmem((MEMBERS, BLOCK, 2 * LANES), BF16),
            vmem((BLOCK, 2048), BF16),
            vmem((MEMBERS, BLOCK, 2 * LANES), BF16),
        ]
        + scatter_scratch(Rows(96, 1024))
        + scatter_scratch(Rows(32, D))
        + wire_scratch(250)
        + [pltpu.SemaphoreType.DMA((20,))],
        2,
        "start",
        63 * 2**20,
    )(parent, table, stream, w_query, w_key, w_value, w_gate, w_up, w_out, small_rows, live_row, cotangent, own_down)


def split_rows(tall, dealt):
    width = dealt.shape[2]
    for member in range(MEMBERS):
        dealt[member] = tall[pl.ds(member * 12, 16), :width].astype(BF16)


def attend_back_kernel(
    lineage, query, live, grad, attended, log_rows, kv_in, grad_query, grad_kv, kv, sums, packed, sems
):
    loaded = pltpu.make_async_copy(kv_in, kv, sems.at[16])
    loaded.start()

    def clear(step, carry):
        sums[step] = jnp.zeros((BLOCK, LANES), F32)
        return carry

    lax.fori_loop(0, 256, clear, 0)
    loaded.wait()

    def two(pair, carry):
        for block in (2 * pair, 2 * pair + 1):
            attend_back_block(block, lineage, query, live, grad, attended, log_rows, grad_query, kv, sums)
        return carry

    lax.fori_loop(0, MEMBERS // 2, two, 0)

    def stored(line):
        rows = pl.ds(line * 12, 12)
        return pltpu.make_async_copy(packed.at[rows], grad_kv.at[rows], sems.at[line])

    def store(line, carry):
        for tile in range(12):
            total = pack_tile(sums[line * 16 + tile], sums[line * 16 + 12 + tile // 3], tile % 3)
            packed[line * 12 + tile] = total.astype(BF16)
        stored(line).start()
        return carry

    lax.fori_loop(0, 16, store, 0)
    for line in range(16):
        stored(line).wait()


def attend_back_block(block, lineage, query, live, grad, attended, log_rows, grad_query, kv, sums):
    across, down_first = (((1,), (1,)), ((), ())), (((0,), (0,)), ((), ()))
    queries = query[block]
    grads = jnp.concatenate([grad[block, :, :LANES], grad[block, :, LANES:]], axis=0)
    outs = jnp.concatenate([attended[block, :, :LANES], attended[block, :, LANES:]], axis=0)
    product = grads.astype(F32) * outs.astype(F32)
    high = product.astype(BF16)
    low = (product - high.astype(F32)).astype(BF16)
    ones = jnp.ones((8, LANES), BF16)
    inner = lax.dot_general(ones, high, across, preferred_element_type=F32)
    inner = (inner + lax.dot_general(ones, low, across, preferred_element_type=F32))[:1]
    logs = log_rows[block, :1]
    limit = count_ancestors(lineage, block)
    u = lax.broadcasted_iota(jnp.int32, (BLOCK, 2 * BLOCK), 0)
    t = lax.broadcasted_iota(jnp.int32, (BLOCK, 2 * BLOCK), 1) % BLOCK
    alive = jnp.transpose(jnp.broadcast_to(live[block], (BLOCK, BLOCK)))
    alive = jnp.concatenate([alive, alive], axis=1)
    own = jnp.logical_and(u <= t, jnp.logical_or(alive > 0.5, u == t))
    turned = jnp.zeros((LANES, 2 * BLOCK), F32)
    for step in range(0, DEPTH, 2):
        units = []
        for node in (lineage[block, step], lineage[block, step + 1]):
            safe = jnp.maximum(node, 0)
            at, member = lax.div(safe, 8) * 16, lax.rem(safe, 8)
            units.append((node, at + key_unit(member), at + value_unit(member)))
        keys = jnp.concatenate([kv[unit[1]] for unit in units], axis=0)
        values = jnp.concatenate([kv[unit[2]] for unit in units], axis=0)
        scores = lax.dot_general(keys, queries, across, preferred_element_type=F32) * SCALE
        near, far = scores[:BLOCK], scores[BLOCK:]
        if step == 0:
            near = jnp.where(own, jnp.exp(jnp.where(own, near - logs, NEGATIVE)), 0.0)
        else:
            near = jnp.exp(near + (jnp.where(step < limit, 0.0, NEGATIVE) - logs))
        far = jnp.exp(far + (jnp.where(step + 1 < limit, 0.0, NEGATIVE) - logs))
        chances = jnp.concatenate([near, far], axis=0)
        grad_chances = lax.dot_general(values, grads, across, preferred_element_type=F32)
        grad_scores = (chances * (grad_chances - inner)).astype(BF16)
        grad_keys = jnp.dot(grad_scores, queries, preferred_element_type=F32) * SCALE
        grad_values = jnp.dot(chances.astype(BF16), grads, preferred_element_type=F32)
        for part, (node, at_key, at_value) in enumerate(units):
            rows = slice(part * BLOCK, (part + 1) * BLOCK)
            sums[jnp.where(node >= 0, at_key, 256)] += grad_keys[rows]
            sums[jnp.where(node >= 0, at_value, 256)] += grad_values[rows]
        turned = turned + lax.dot_general(keys, grad_scores, down_first, preferred_element_type=F32)
    grad_query[block] = jnp.transpose(turned) * SCALE


def attend_back(lineage, query, kv, live, grad, attended, log_rows):
    vmem = pltpu.VMEM
    return pl.pallas_call(
        attend_back_kernel,
        in_specs=[pl.BlockSpec(memory_space=pltpu.SMEM)] + [INVMEM] * 5 + [ANY],
        out_specs=(INVMEM, ANY),
        out_shape=(
            jax.ShapeDtypeStruct((MEMBERS, 2 * BLOCK, LANES), F32),
            jax.ShapeDtypeStruct((192, BLOCK, LANES), BF16),
        ),
        scratch_shapes=[
            vmem((256, BLOCK, LANES), BF16),
            vmem((257, BLOCK, LANES), F32),
            vmem((192, BLOCK, LANES), BF16),
            pltpu.SemaphoreType.DMA((17,)),
        ],
        compiler_params=pltpu.CompilerParams(vmem_limit_bytes=VMEM_BYTES),
        name="attend_back",
    )(lineage, query, live, grad, attended, log_rows, kv)


def gain_tiles(rows):
    lane = lane_of((8, LANES))
    tiles = [rows[:, tile * LANES : (tile + 1) * LANES] for tile in range(12)]
    pieces = []
    for piece in range(16):
        tile, skip = divmod(piece * 96, LANES)
        low = pltpu.roll(tiles[tile], (LANES - skip) % LANES, 1)
        high = pltpu.roll(tiles[min(tile + 1, 11)], (LANES - skip) % LANES, 1)
        pieces.append(jnp.where(lane < LANES - skip, low, high))
    return pieces


def ending_kernel(
    lineage, grad_query, table, stream_all, w_attn, gain, gain_two, stream, middle, grad_middle,
    feed_lines, wide_lines, kv_terms, down_terms, out_terms,
    mixed_out, stream_grad, query_grad, key_grad, value_grad, out_grad, gain_one, gain_two_out, rms_out,
    gate_grad, up_grad, down_grad,
    feed_second, wide_second, feed_tall, feed_dealt, feed_in, attn_grad, out_in, normed, raw, units, grad_terms, crossed_in, near_in, far_in, query_terms, pair_terms, attn_tall, attn_dealt,
    out_tall, out_dealt, out_mine, out_crossed, gain_terms, gain_in, gain_line, gain_in_two, gain_in_three,
    *scratch,
):
    xyzc = x, y, z, c = spot()
    j = z * 2 + c
    down_scratch, kv_scratch, query_scratch, pair_scratch, out_scratch = (
        scratch[:5], scratch[5:13], scratch[13:18], scratch[18:23], scratch[23:28]
    )
    send_sems, recv_sems, local_sem = scratch[28:]
    wire = Wire(send_sems, recv_sems)
    group = [group_peer(x, y, z, c, k) for k in range(1, MEMBERS)]
    peers = group + axis_peers(x, y, z, c, True)
    announce(peers)
    await_peers(peers)
    sibling = device_of(x, y, z, 1 - c)
    pairs = PlaneScatter(wire, kv_terms, Units(), kv_scratch, xyzc)
    pairs.first()
    attn_tall[96:] = jnp.zeros((8, 512), F32)
    feed_tall[96:] = jnp.zeros((8, 1024), F32)
    out_tall[96:] = jnp.zeros((8, 768), F32)

    def norm_rows(step, carry):
        rows = pl.ds(pl.multiple_of(step * BLOCK, BLOCK), BLOCK)
        wide = stream_all[rows].astype(F32)
        rms = jnp.sqrt(jnp.mean(wide * wide, axis=1, keepdims=True) + EPSILON)
        normed[rows] = (wide * (1.0 / rms) * gain[0:1]).astype(BF16)
        return carry

    lax.fori_loop(0, MEMBERS, norm_rows, 0)

    def turn(block, v):
        depth = count_ancestors(lineage, block) - 1
        cos, sin = turning(table[depth])
        return (v * cos - swap_halves(v) * sin).astype(BF16)

    def query_rows(block, carry):
        rows = pl.ds(pl.multiple_of(block * BLOCK, BLOCK), BLOCK)
        raw[rows, :128] = turn(block, grad_query[block, :BLOCK])
        raw[rows, 128:256] = turn(block, grad_query[block, BLOCK:])
        return carry

    lax.fori_loop(0, MEMBERS, query_rows, 0)
    pairs.relay()
    downs = GroupScatter(wire, down_terms, *down_scratch, xyzc)
    downs.begin()
    own_half = pl.ds(pl.multiple_of(c * 768, 768), 768)
    other_half = pl.ds(pl.multiple_of((1 - c) * 768, 768), 768)
    crossed = wire.send(out_terms.at[:, :, :, other_half], out_crossed, sibling)
    local = pltpu.make_async_copy(out_terms.at[:, :, :, own_half], out_mine, local_sem)
    local.start()

    def weights_back(terms, first):
        def some(step, carry):
            cols = pl.ds(pl.multiple_of(step * 384, 384), 384)
            total = lax.dot_general(
                normed[:, cols], raw[:, first : first + 256], (((0,), (0,)), ((), ())), preferred_element_type=F32
            )
            terms[step] = total.astype(BF16).reshape(4, 96, 256)
            return carry

        lax.fori_loop(0, 4, some, 0)

    weights_back(query_terms, 0)
    query_sums = PlaneScatter(wire, query_terms, Rows(96, 256), query_scratch, xyzc)
    pair_sums = PlaneScatter(wire, pair_terms, Rows(96, 256), pair_scratch, xyzc)
    local.wait()
    crossed.wait_recv()

    def add_halves(step, carry):
        a, b = step // 4, step % 4
        total = out_mine[a, b].astype(F32) + out_crossed[a, b].astype(F32)
        out_mine[a, b] = total.astype(BF16)
        return carry

    lax.fori_loop(0, 16, add_halves, 0)
    outs = PlaneScatter(wire, out_mine, Rows(96, 768), out_scratch, xyzc)
    downs.turn()
    pairs.add_first()
    pairs.second()
    downs.finish(stream_grad)
    mixed_out[...] = (middle[...] + stream_grad[...]).astype(BF16)
    pairs.arrive()
    outs.first()
    query_sums.first()
    for half in range(2):
        units[pl.ds(half * 6, 6)] = pairs.total(half)
    for extra in range(4):
        units[12 + extra] = unpack_extra([units[extra * 3 + k] for k in range(3)])

    def pair_rows(block, carry):
        rows = pl.ds(pl.multiple_of(block * BLOCK, BLOCK), BLOCK)
        raw[rows, 256:384] = turn(block, units[key_unit(block)])
        value = units[value_unit(block)]
        raw[rows, 384:] = jnp.where(lane_of((BLOCK, LANES)) < HEAD_DIM, value, 0.0).astype(BF16)
        return carry

    lax.fori_loop(0, MEMBERS, pair_rows, 0)

    grad_rows = RingScatter(wire, grad_terms, crossed_in, near_in, far_in, xyzc)
    gain_terms[...] = jnp.zeros((1, D), F32)

    def rows_back(step):
        rows = pl.ds(pl.multiple_of(grad_rows.place(step) * 256, 256), 256)
        grads = lax.dot_general(raw[rows], w_attn[...], (((1,), (1,)), ((), ())), preferred_element_type=F32)
        grad_rows.put(step, grads.astype(BF16))
        wide = stream_all[rows].astype(F32)
        rms = jnp.sqrt(jnp.mean(wide * wide, axis=1, keepdims=True) + EPSILON)
        gain_terms[...] += jnp.sum(grads * (wide * (1.0 / rms)), axis=0, keepdims=True)

    rows_back(2)
    rows_back(1)
    grad_rows.turn(2)
    rows_back(3)
    grad_rows.turn(1)
    rows_back(0)
    grad_rows.turn(3)
    outs.relay()
    query_sums.relay()
    grad_rows.pass_on(1)
    grad_rows.pass_on(3)
    rows = jnp.concatenate([gain_terms[...], gain_two[...], jnp.zeros((6, D), F32)], axis=0)
    for piece, part in enumerate(gain_tiles(rows)):
        gain_in[piece // 4, piece % 4] = part
    gains = [
        wire.send(gain_in.at[(x + k) % 4], gain_line.at[k], device_of(x + k, y, z, c)) for k in range(1, 4)
    ]

    weights_back(pair_terms, 256)
    pair_sums.first()
    for copy in gains:
        copy.wait_recv()
    gain_line[0] = gain_in[x] + gain_line[1] + gain_line[2] + gain_line[3]
    gains = [
        wire.send(gain_line.at[0, (y + k) % 4], gain_in_two.at[k], device_of(x, y + k, z, c)) for k in range(1, 4)
    ]
    outs.add_first()
    outs.second()
    query_sums.add_first()
    query_sums.second()
    pair_sums.relay()
    outs.arrive()
    for half in range(2):
        out_tall[pl.ds(half * 48, 48)] = outs.total(half)
    split_rows(out_tall, out_dealt)
    out_in[j] = out_dealt[j]
    dealt = [
        wire.send(out_dealt.at[(j + k) % MEMBERS], out_in.at[j], group[k - 1]) for k in range(1, MEMBERS)
    ]
    pair_sums.add_first()
    pair_sums.second()
    feeds = SecondRound(wire, feed_lines, feed_second, xyzc)
    wides = SecondRound(wire, wide_lines, wide_second, xyzc)
    feeds.second()
    wides.second()

    wide = stream[...].astype(F32)
    rms = jnp.sqrt(jnp.mean(wide * wide, axis=1, keepdims=True) + EPSILON)
    rms_out[...] = jnp.transpose(jnp.broadcast_to(rms, (BLOCK, LANES)))[:1]
    scaled = wide / rms
    weighted = grad_rows.total() * gain[0:1]
    back = (weighted - scaled * jnp.mean(weighted * scaled, axis=1, keepdims=True)) / rms
    stream_grad[...] = grad_middle[...] + back

    for copy in gains:
        copy.wait_recv()
    gain_in_three[j] = gain_line[0, y] + gain_in_two[1] + gain_in_two[2] + gain_in_two[3]
    gains = [
        wire.send(gain_in_three.at[j], gain_in_three.at[j], group[k - 1]) for k in range(1, MEMBERS)
    ]
    query_sums.arrive()
    pair_sums.arrive()
    for half in range(2):
        attn_tall[pl.ds(half * 48, 48), :256] = query_sums.total(half)
        attn_tall[pl.ds(half * 48, 48), 256:] = pair_sums.total(half)
    split_rows(attn_tall, attn_dealt)
    attn_grad[j] = attn_dealt[j]
    dealt += [
        wire.send(attn_dealt.at[(j + k) % MEMBERS], attn_grad.at[j], group[k - 1]) for k in range(1, MEMBERS)
    ]
    feeds.arrive()
    for half in range(2):
        feed_tall[pl.ds(half * 48, 48)] = feeds.total(half)
    split_rows(feed_tall, feed_dealt)
    feed_in[j] = feed_dealt[j]
    feed_copies = [
        wire.send(feed_dealt.at[(j + k) % MEMBERS], feed_in.at[j], group[k - 1]) for k in range(1, MEMBERS)
    ]
    wides.arrive()
    for half in range(2):
        down_grad[pl.ds(half * 16, 16)] = wides.total(half)
    for copy in gains:
        copy.wait_recv()
    total = gain_in_three[0]
    for member in range(1, MEMBERS):
        total = total + gain_in_three[member]
    own = pltpu.roll(total, (LANES - 12 * j) % LANES, 1)
    gain_one[...] = own[:1, :12]
    gain_two_out[...] = own[1:2, :12]
    for copy in dealt:
        copy.wait_recv()
    for core in range(2):
        total = out_in[core].astype(F32)
        for place in range(1, 4):
            total = total + out_in[place * 2 + core].astype(F32)
        out_grad[:, core * 768 : (core + 1) * 768] = total[:12]

    def tile_of(member, tile):
        return attn_grad[member, :, tile * LANES : (tile + 1) * LANES].astype(F32)

    for grad, pieces in (
        (query_grad, [tile_of(head // 2, head % 2) for head in range(HEADS)]),
        (key_grad, [tile_of(member, 2) for member in range(MEMBERS)]),
        (value_grad, [tile_of(member, 3) for member in range(MEMBERS)]),
    ):
        for tile, value in enumerate(join_heads(pieces)):
            grad[:, tile * LANES : (tile + 1) * LANES] = value[:12]
    for copy in feed_copies:
        copy.wait_recv()
    for grad, first in ((gate_grad, 0), (up_grad, 4)):
        for tile in range(32):
            line = tile // 2
            cols = slice((first + line // 4) * LANES, (first + line // 4 + 1) * LANES)
            parts = [(feed_in[4 * (tile % 2) + i, :, cols].astype(F32), line % 4) for i in range(4)]
            grad[:, tile * LANES : (tile + 1) * LANES] = mix_groups(parts)[:12]
    wire.close()
    grad_rows.close()


def ending(
    lineage, grad_query, table, stream_all, w_attn, gain, gain_two, stream, middle, grad_middle,
    feed_lines, wide_lines, kv_terms, down_terms, out_terms,
):
    shape, vmem = jax.ShapeDtypeStruct, pltpu.VMEM
    smem = pl.BlockSpec(memory_space=pltpu.SMEM)
    return communicate(
        ending_kernel,
        (
            shape((BLOCK, D), BF16),
            shape((BLOCK, D), F32),
            shape((12, D), F32),
            shape((12, 768), F32),
            shape((12, 768), F32),
            shape((12, D), F32),
            shape((1, 12), F32),
            shape((1, 12), F32),
            shape((1, LANES), F32),
            shape((12, FF), F32),
            shape((12, FF), F32),
            shape((32, D), F32),
        ),
        [smem] + [INVMEM] * 11 + [ANY] * 3,
        (INVMEM,) * 12,
        [
            vmem((2, 3, 48, 1024), BF16),
            vmem((2, 3, 16, D), BF16),
            vmem((104, 1024), F32),
            vmem((MEMBERS, 16, 1024), BF16),
            vmem((MEMBERS, 16, 1024), BF16),
            vmem((MEMBERS, 16, 512), BF16),
            vmem((MEMBERS, 16, 768), BF16),
            vmem((MEMBERS * BLOCK, D), BF16),
            vmem((MEMBERS * BLOCK, 512), BF16),
            vmem((16, BLOCK, LANES), F32),
            vmem((4, 2, 12, BLOCK, LANES), BF16),
        ]
        + [
            vmem((4, 12, BLOCK, LANES), BF16),
            vmem((2, 12, BLOCK, LANES), BF16),
            vmem((2, 6, BLOCK, LANES), BF16),
        ]
        + [
            vmem((4, 4, 96, 256), BF16),
            vmem((4, 4, 96, 256), BF16),
            vmem((104, 512), F32),
            vmem((MEMBERS, 16, 512), BF16),
            vmem((104, 768), F32),
            vmem((MEMBERS, 16, 768), BF16),
            vmem((4, 4, 96, 768), BF16),
            vmem((4, 4, 96, 768), BF16),
            vmem((1, D), F32),
            vmem((4, 4, 8, LANES), F32),
            vmem((4, 4, 8, LANES), F32),
            vmem((4, 8, LANES), F32),
            vmem((MEMBERS, 8, LANES), F32),
        ]
        + group_scatter_scratch()
        + scatter_scratch(Units(), room=True)
        + scatter_scratch(Rows(96, 256))
        + scatter_scratch(Rows(96, 256))
        + scatter_scratch(Rows(96, 768))
        + wire_scratch(140)
        + [pltpu.SemaphoreType.DMA],
        7,
        "ending",
        62 * 2**20,
    )(
        lineage, grad_query, table, stream_all, w_attn, gain, gain_two, stream, middle, grad_middle,
        feed_lines, wide_lines, kv_terms, down_terms, out_terms,
    )


def hand_over_kernel(*refs):
    count = len(refs) // 2
    for source, target in zip(refs[:count], refs[count:]):
        target[...] = source[...]


def hand_over(*arrays):
    return pl.pallas_call(
        hand_over_kernel,
        out_shape=tuple(jax.ShapeDtypeStruct(array.shape, array.dtype) for array in arrays),
        in_specs=[INVMEM] * len(arrays),
        out_specs=(INVMEM,) * len(arrays),
        compiler_params=pltpu.CompilerParams(vmem_limit_bytes=VMEM_BYTES),
        name="hand_over",
    )(*arrays)


def shards(
    stream, attn_gain, w_query, w_key, w_value, w_out, mlp_gain, w_gate, w_up, w_down, parent, live_mask, cotangent
):
    table = rope_table()
    small_rows = jnp.pad(jnp.stack([attn_gain, mlp_gain]).astype(F32), ((0, 6), (0, LANES - attn_gain.shape[0])))
    (
        lineage, live, gains, query, stream_all, w_attn, context, middle, branch_rms, grad_middle, grad_heads,
        down_terms, feed_lines, wide_lines, out_terms, gain_two_terms, attended, log_rows,
    ) = start(
        parent, table, stream, w_query, w_key, w_value, w_gate, w_up, w_out, small_rows,
        live_mask.reshape(1, BLOCK), cotangent, w_down,
    )
    grad_query, context_terms = attend_back(
        lineage, query, context.reshape(256, BLOCK, LANES), live, grad_heads, attended, log_rows
    )
    (
        mixed_out, stream_grad, query_grad, key_grad, value_grad, out_grad, gain_one, gain_two, stream_rms,
        gate_grad, up_grad, down_grad,
    ) = ending(
        lineage, grad_query, table, stream_all.reshape(MEMBERS * BLOCK, D), w_attn.reshape(D, 512), gains,
        gain_two_terms, stream, middle, grad_middle, feed_lines, wide_lines,
        context_terms.reshape(4, 4, 12, BLOCK, LANES), down_terms, out_terms,
    )
    (
        mixed_out, stream_grad, gain_one, query_grad, key_grad, value_grad, out_grad, gain_two,
        gate_grad, up_grad, down_grad, stream_rms, branch_rms,
    ) = hand_over(
        mixed_out, stream_grad, gain_one, query_grad, key_grad, value_grad, out_grad, gain_two,
        gate_grad, up_grad, down_grad, stream_rms, branch_rms,
    )
    return (
        mixed_out, stream_grad, gain_one[0], query_grad, key_grad, value_grad, out_grad, gain_two[0],
        gate_grad, up_grad, down_grad, stream_rms[0], branch_rms[0],
    )


def solution(mesh):
    rows, line = P("dev", None), P("dev")
    return jax.shard_map(
        shards,
        mesh=mesh,
        in_specs=(rows, line, rows, rows, rows, rows, line, rows, rows, rows, P(), line, rows),
        out_specs=(rows, rows, line, rows, rows, rows, rows, line, rows, rows, rows, line, line),
        check_vma=False,
    )
```

profile of v0, /device:TPU:1, one launch (start us, length us, event | category | flops | bytes accessed | tf_op | source)
XLA Modules:
  0.0 269.5 jit_solution(2293107228078807788)
XLA Ops:
  0.6 1.3 fusion.6.small_rows
  1.9 156.9 %start.1 = (s32[8,10]{1,0:T(8,128)}, f32[8,1,128]{2,1,0:T(1,128)}, f32[8,1536]{1,0:T(8,128)}, bf16[8,256,128]{2,1,0:T(8,128)(2,1)}, bf16[4,2,128,1536]{3,2,1,0:T...) custom-call(s32[128]{0:T(128)} %parent.1, ...), custom_call_target="tpu_custom_call" | custom-call | tf_op jit(solution)/shard_map/start/pallas_call | solution.py:1197
  158.8 20.7 %attend_back.1 = (f32[8,256,128]{2,1,0:T(8,128)}, bf16[192,128,128]{2,1,0:T(8,128)(2,1)}) custom-call(s32[8,10]{1,0:T(8,128)} %get-tuple-element.58.lineage, bf16[8,256,128]{2,1,0:T(8,128)(2,1)} %get-tuple-element.59.query, f32[8,1,128]{2,1,0:T(1,128)} %get-tuple-element.60.live, bf16[8,128,256]{2,1,0:T(8,128)(2,1)} %get-tuple-element.61.grad, ...), custom_call_target="tpu_custom_call" | custom-call | tf_op jit(solution)/shard_map/attend_back/pallas_call | solution.py:1351
  179.6 86.8 %ending.1 = (bf16[128,1536]{1,0:T(8,128)(2,1)}, f32[128,1536]{1,0:T(8,128)}, f32[12,1536]{1,0:T(8,128)}, f32[12,768]{1,0:T(8,128)}, f32[12,768]{1,0:T(8,128)}, /...) custom-call(s32[8,10]{1,0:T(8,128)} %get-tuple-element.58.lineage, ...), custom_call_target="tpu_custom_call" | custom-call | tf_op jit(solution)/shard_map/ending/pallas_call | solution.py:1622
  266.3 3.0 %hand_over.1 = (bf16[128,1536]{1,0:T(8,128)(2,1)}, f32[128,1536]{1,0:T(8,128)}, f32[1,12]{1,0:T(1,128)}, f32[12,1536]{1,0:T(8,128)}, f32[12,768]{1,0:T(8,128)}, ...) custom-call(bf16[128,1536]{1,0:T(8,128)(2,1)} %get-tuple-element.77., ...), custom_call_target="tpu_custom_call" | custom-call | tf_op jit(solution)/shard_map/hand_over/pallas_call | solution.py:1696
where the time goes:
time: 270 us; the launch traced here: 269 us
  Pallas kernels  267 us (99%)
    pallas_call x1, Pallas kernels, start(): communicate(start_kernel, (shape((MEMBERS, DEPTH), jnp.int32), shape((MEM...  157 us
    pallas_call x1, Pallas kernels, ending(): communicate(ending_kernel, (shape((BLOCK, D), BF16), shape((BLOCK, D), F3...  86.8 us
    pallas_call x1, Pallas kernels, attend_back(): pl.pallas_call(attend_back_kernel, in_specs=[pl.BlockSpec(memory_space=pl...  20.7 us

commit v1 on v0

--- a/solution.py
+++ b/solution.py
@@ -1469,6 +1469,10 @@
     pairs.arrive()
     outs.first()
     query_sums.first()
+    feeds = SecondRound(wire, feed_lines, feed_second, xyzc)
+    wides = SecondRound(wire, wide_lines, wide_second, xyzc)
+    feeds.second()
+    wides.second()
     for half in range(2):
         units[pl.ds(half * 6, 6)] = pairs.total(half)
     for extra in range(4):
@@ -1533,12 +1537,19 @@
     dealt = [
         wire.send(out_dealt.at[(j + k) % MEMBERS], out_in.at[j], group[k - 1]) for k in range(1, MEMBERS)
     ]
+    feeds.arrive()
+    for half in range(2):
+        feed_tall[pl.ds(half * 48, 48)] = feeds.total(half)
+    split_rows(feed_tall, feed_dealt)
+    feed_in[j] = feed_dealt[j]
+    feed_copies = [
+        wire.send(feed_dealt.at[(j + k) % MEMBERS], feed_in.at[j], group[k - 1]) for k in range(1, MEMBERS)
+    ]
+    wides.arrive()
+    for half in range(2):
+        down_grad[pl.ds(half * 16, 16)] = wides.total(half)
     pair_sums.add_first()
     pair_sums.second()
-    feeds = SecondRound(wire, feed_lines, feed_second, xyzc)
-    wides = SecondRound(wire, wide_lines, wide_second, xyzc)
-    feeds.second()
-    wides.second()
 
     wide = stream[...].astype(F32)
     rms = jnp.sqrt(jnp.mean(wide * wide, axis=1, keepdims=True) + EPSILON)
@@ -1564,17 +1575,6 @@
     dealt += [
         wire.send(attn_dealt.at[(j + k) % MEMBERS], attn_grad.at[j], group[k - 1]) for k in range(1, MEMBERS)
     ]
-    feeds.arrive()
-    for half in range(2):
-        feed_tall[pl.ds(half * 48, 48)] = feeds.total(half)
-    split_rows(feed_tall, feed_dealt)
-    feed_in[j] = feed_dealt[j]
-    feed_copies = [
-        wire.send(feed_dealt.at[(j + k) % MEMBERS], feed_in.at[j], group[k - 1]) for k in range(1, MEMBERS)
-    ]
-    wides.arrive()
-    for half in range(2):
-        down_grad[pl.ds(half * 16, 16)] = wides.total(half)
     for copy in gains:
         copy.wait_recv()
     total = gain_in_three[0]
@@ -1583,24 +1583,6 @@
     own = pltpu.roll(total, (LANES - 12 * j) % LANES, 1)
     gain_one[...] = own[:1, :12]
     gain_two_out[...] = own[1:2, :12]
-    for copy in dealt:
-        copy.wait_recv()
-    for core in range(2):
-        total = out_in[core].astype(F32)
-        for place in range(1, 4):
-            total = total + out_in[place * 2 + core].astype(F32)
-        out_grad[:, core * 768 : (core + 1) * 768] = total[:12]
-
-    def tile_of(member, tile):
-        return attn_grad[member, :, tile * LANES : (tile + 1) * LANES].astype(F32)
-
-    for grad, pieces in (
-        (query_grad, [tile_of(head // 2, head % 2) for head in range(HEADS)]),
-        (key_grad, [tile_of(member, 2) for member in range(MEMBERS)]),
-        (value_grad, [tile_of(member, 3) for member in range(MEMBERS)]),
-    ):
-        for tile, value in enumerate(join_heads(pieces)):
-            grad[:, tile * LANES : (tile + 1) * LANES] = value[:12]
     for copy in feed_copies:
         copy.wait_recv()
     for grad, first in ((gate_grad, 0), (up_grad, 4)):
@@ -1609,6 +1591,24 @@
             cols = slice((first + line // 4) * LANES, (first + line // 4 + 1) * LANES)
             parts = [(feed_in[4 * (tile % 2) + i, :, cols].astype(F32), line % 4) for i in range(4)]
             grad[:, tile * LANES : (tile + 1) * LANES] = mix_groups(parts)[:12]
+    for copy in dealt:
+        copy.wait_recv()
+    for core in range(2):
+        total = out_in[core].astype(F32)
+        for place in range(1, 4):
+            total = total + out_in[place * 2 + core].astype(F32)
+        out_grad[:, core * 768 : (core + 1) * 768] = total[:12]
+
+    def tile_of(member, tile):
+        return attn_grad[member, :, tile * LANES : (tile + 1) * LANES].astype(F32)
+
+    for grad, pieces in (
+        (query_grad, [tile_of(head // 2, head % 2) for head in range(HEADS)]),
+        (key_grad, [tile_of(member, 2) for member in range(MEMBERS)]),
+        (value_grad, [tile_of(member, 3) for member in range(MEMBERS)]),
+    ):
+        for tile, value in enumerate(join_heads(pieces)):
+            grad[:, tile * LANES : (tile + 1) * LANES] = value[:12]
     wire.close()
     grad_rows.close()
 

time: 270 us -> 271 us (level)
  no operation moved by 1% of the time
where the time goes in v1:
time: 271 us; the launch traced here: 270 us
  Pallas kernels  268 us (99%)
    pallas_call x1, Pallas kernels, start(): communicate(start_kernel, (shape((MEMBERS, DEPTH), jnp.int32), shape((MEM...  157 us
    pallas_call x1, Pallas kernels, ending(): communicate(ending_kernel, (shape((BLOCK, D), BF16), shape((BLOCK, D), F3...  87.8 us
    pallas_call x1, Pallas kernels, attend_back(): pl.pallas_call(attend_back_kernel, in_specs=[pl.BlockSpec(memory_space=pl...  20.7 us

profile of v1, /device:TPU:1, one launch (start us, length us, event | category | flops | bytes accessed | tf_op | source)
XLA Modules:
  0.0 270.5 jit_solution(7232722254404735753)
XLA Ops:
  0.6 1.3 fusion.6.small_rows
  1.9 156.9 %start.1 = (s32[8,10]{1,0:T(8,128)}, f32[8,1,128]{2,1,0:T(1,128)}, f32[8,1536]{1,0:T(8,128)}, bf16[8,256,128]{2,1,0:T(8,128)(2,1)}, bf16[4,2,128,1536]{3,2,1,0:T...) custom-call(s32[128]{0:T(128)} %parent.1, ...), custom_call_target="tpu_custom_call" | custom-call | tf_op jit(solution)/shard_map/start/pallas_call | solution.py:1197
  158.8 20.7 %attend_back.1 = (f32[8,256,128]{2,1,0:T(8,128)}, bf16[192,128,128]{2,1,0:T(8,128)(2,1)}) custom-call(s32[8,10]{1,0:T(8,128)} %get-tuple-element.58.lineage, bf16[8,256,128]{2,1,0:T(8,128)(2,1)} %get-tuple-element.59.query, f32[8,1,128]{2,1,0:T(1,128)} %get-tuple-element.60.live, bf16[8,128,256]{2,1,0:T(8,128)(2,1)} %get-tuple-element.61.grad, ...), custom_call_target="tpu_custom_call" | custom-call | tf_op jit(solution)/shard_map/attend_back/pallas_call | solution.py:1351
  179.6 87.8 %ending.1 = (bf16[128,1536]{1,0:T(8,128)(2,1)}, f32[128,1536]{1,0:T(8,128)}, f32[12,1536]{1,0:T(8,128)}, f32[12,768]{1,0:T(8,128)}, f32[12,768]{1,0:T(8,128)}, /...) custom-call(s32[8,10]{1,0:T(8,128)} %get-tuple-element.58.lineage, ...), custom_call_target="tpu_custom_call" | custom-call | tf_op jit(solution)/shard_map/ending/pallas_call | solution.py:1622
  267.3 3.0 %hand_over.1 = (bf16[128,1536]{1,0:T(8,128)(2,1)}, f32[128,1536]{1,0:T(8,128)}, f32[1,12]{1,0:T(1,128)}, f32[12,1536]{1,0:T(8,128)}, f32[12,768]{1,0:T(8,128)}, ...) custom-call(bf16[128,1536]{1,0:T(8,128)(2,1)} %get-tuple-element.77., ...), custom_call_target="tpu_custom_call" | custom-call | tf_op jit(solution)/shard_map/hand_over/pallas_call | solution.py:1696
